TPU v7x, 128 devices: a whole 4x4x4 slice. The times are simulated.
128 devices in a mesh: bl: 16 (over x, y_hi, core), ch: 8 (over z, y_lo).
Axes of the slice: x: 4, y: 4 (y_hi: 2, y_lo: 2; y = y_hi * 2 + y_lo), z: 4, core: 2. Of those that a mesh axis runs over, the one named last changes fastest.
Arguments:
- uvw_index: int32 [2048], P('bl'), may hold values from 0 to 4095
- row_baseline: int32 [2048], P('bl'), may hold values from 0 to 2015
- flags: int32 [2048, 256], P('bl', 'ch'), may hold values 0 or 1
- uvw_table: bfloat16 [64, 4096], replicated, may hold values from -6 to 6
- baseline_features: bfloat16 [64, 2016], replicated, may hold values from -6 to 6
- w_in: bfloat16 [64, 64], replicated, may hold values from -0.75 to 0.75
- w_out: bfloat16 [64, 2, 65536], P(None, None, 'ch'), may hold values from -0.75 to 0.75
- observed: bfloat16 [2, 65536, 2048], P(None, 'ch', 'bl'), may hold values from -6 to 6
- delay_weight: float32 [65536], replicated, may hold values from 0.25 to 4
Outputs:
- grad_out: float32 [64, 2, 65536], P('bl', None, 'ch')
- grad_in: float32 [64, 64], replicated
- grad_uvw: float32 [64, 4096], replicated
- grad_base: float32 [64, 2016], replicated
All inputs are finite; a program needn't handle non-finite values. No bound on the sum of `flags` on one device may be relied on, other than what follows from the above.
Results may differ from a plain program's by a relative error of at most 0.00035.
The roundings to bfloat16 on the way count: a program that leaves them out, or rounds other values in their place, can miss the bound.
Values sent between devices are 32-bit elements; how exact they have to be, the bound alone decides.
No kernel may reach another device: no remote copies, remote signals or barrier semaphores. Data moves between devices by JAX's collectives and lax.ppermute only.
A program may use at most 128 MiB of HBM per device.

v0:
```python
import math

import jax
import jax.numpy as jnp
from jax import lax
from jax.sharding import PartitionSpec as P

BLOCK = 256
NBLOCKS = 256
CHANNELS = 65536


loss_scale = 0.0625
highest = lax.Precision.HIGHEST


def angle_of(product, period):
    return (product % period).astype(jnp.float32) * (2.0 * math.pi / period)


def taper_values(offset, length):
    channel_number = offset + lax.broadcasted_iota(jnp.int32, (length,), 0)
    window = jnp.full((length,), 0.35875, jnp.float32)
    for harmonic, weight_term in ((1, -0.48829), (2, 0.14128), (3, -0.01168)):
        window = window + weight_term * jnp.cos(angle_of(channel_number * harmonic, CHANNELS))
    return window


def dft_pair(length, sign):
    row_index = lax.broadcasted_iota(jnp.int32, (length, length), 0)
    col_index = lax.broadcasted_iota(jnp.int32, (length, length), 1)
    phases = angle_of(row_index * col_index, length)
    cosine = jnp.cos(phases)
    sine_part = sign * jnp.sin(phases)
    return jnp.stack([jnp.stack([cosine, sine_part]), jnp.stack([-sine_part, cosine])])


def rotate(values, cosine, sine_part):
    real_part = values[0] * cosine - values[1] * sine_part
    imag_part = values[1] * cosine + values[0] * sine_part
    return jnp.stack([real_part, imag_part])


def spectral(
    blocks, delay_weight, row_groups, position, members, move_in, move_mid, move_back, move_out
):
    row_count = blocks.shape[-1]
    local_blocks = blocks.shape[2]
    k_width = BLOCK // members
    t_width = NBLOCKS // members
    owners = members // row_groups
    arrived = move_in(blocks).reshape(2, row_groups, owners, local_blocks, k_width, row_count)
    first_matrix = dft_pair(NBLOCKS, -1.0).reshape(2, 2, owners, local_blocks, NBLOCKS)
    first_section = jnp.einsum("pacbkr,pqcbt->qatkr", arrived, first_matrix, precision=highest)
    t_all = lax.broadcasted_iota(jnp.int32, (NBLOCKS, k_width), 0)
    k_part = position * k_width + lax.broadcasted_iota(jnp.int32, (NBLOCKS, k_width), 1)
    phases = angle_of(t_all * k_part, CHANNELS)
    first_section = rotate(
        first_section, jnp.cos(phases)[None, :, :, None], -jnp.sin(phases)[None, :, :, None]
    )
    turned = move_mid(first_section)
    second = jnp.einsum("patkr,pqks->qatsr", turned, dft_pair(BLOCK, -1.0), precision=highest)
    t_part = position * t_width + lax.broadcasted_iota(jnp.int32, (t_width, BLOCK), 0)
    s_all = lax.broadcasted_iota(jnp.int32, (t_width, BLOCK), 1)
    weight_grid = delay_weight.reshape(BLOCK, NBLOCKS)
    picked = lax.dynamic_slice_in_dim(weight_grid, position * t_width, t_width, 1).T
    factor = picked * (loss_scale / CHANNELS)
    scaled = second * factor[None, None, :, :, None]
    third_section = jnp.einsum("patsr,pqsk->qatkr", scaled, dft_pair(BLOCK, 1.0), precision=highest)
    phases_back = angle_of(t_part * s_all, CHANNELS)
    third_section = rotate(
        third_section,
        jnp.cos(phases_back)[None, :, :, None],
        jnp.sin(phases_back)[None, :, :, None],
    )
    returned = move_back(third_section)
    last_matrix = dft_pair(NBLOCKS, 1.0).reshape(2, 2, NBLOCKS, owners, local_blocks)
    fourth = jnp.einsum("patkr,pqtcb->qacbkr", returned, last_matrix, precision=highest)
    fourth = fourth.reshape(2, members, local_blocks, k_width, row_count)
    restored = move_out(fourth)
    return restored.reshape(2, local_blocks * BLOCK, row_count)


def trunk_grads(hidden_grad, pre_act, inputs, w_in, cell_pick, base_pick):
    sigmoid_part = jax.nn.sigmoid(pre_act)
    pre_grad = hidden_grad * sigmoid_part * (1.0 + pre_act * (1.0 - sigmoid_part))
    grad_in = jnp.dot(inputs.astype(jnp.float32), pre_grad.T, precision=highest)
    input_grad = jnp.dot(w_in.astype(jnp.float32), pre_grad, precision=highest)
    grad_uvw = jnp.dot(input_grad, cell_pick.T, precision=highest)
    grad_base = jnp.dot(input_grad, base_pick.T, precision=highest)
    return (grad_in, grad_uvw, grad_base)


def over_rows(grad_in, grad_uvw, grad_base):
    return lax.psum((grad_in, grad_uvw, grad_base), "bl")


def body(
    uvw_index,
    row_baseline,
    flags,
    uvw_table,
    baseline_features,
    w_in,
    w_out,
    observed,
    delay_weight,
):
    row_count = uvw_index.shape[0]
    local_blocks = flags.shape[1]
    local_channels = w_out.shape[2]
    cell_pick = (
        lax.broadcasted_iota(jnp.int32, (uvw_table.shape[1], row_count), 0) == uvw_index[None, :]
    ).astype(jnp.float32)
    base_pick = (
        lax.broadcasted_iota(jnp.int32, (baseline_features.shape[1], row_count), 0)
        == row_baseline[None, :]
    ).astype(jnp.float32)
    summed = jnp.dot(uvw_table, cell_pick.astype(jnp.bfloat16), preferred_element_type=jnp.float32)
    summed = summed + jnp.dot(
        baseline_features, base_pick.astype(jnp.bfloat16), preferred_element_type=jnp.float32
    )
    inputs = summed.astype(jnp.bfloat16)
    pre_act = lax.dot_general(
        w_in, inputs, (((0,), (0,)), ((), ())), preferred_element_type=jnp.float32
    )
    hidden = jax.nn.silu(pre_act).astype(jnp.bfloat16)
    field = jnp.einsum("jqc,jr->qcr", w_out, hidden, preferred_element_type=jnp.float32)
    offset = lax.axis_index("ch") * local_channels
    taper = taper_values(offset, local_channels)
    kept_share = 1.0 - flags.astype(jnp.float32)
    weight = (kept_share.T[:, None, :] * taper.reshape(local_blocks, BLOCK)[:, :, None]).reshape(
        local_channels, row_count
    )
    residual_vis = (field - observed.astype(jnp.float32)) * weight[None]
    blocks = residual_vis.reshape(2, 1, local_blocks, BLOCK, row_count)
    gradient = spectral(
        blocks,
        delay_weight,
        lax.axis_size("bl"),
        lax.axis_index(("bl", "ch")),
        lax.axis_size(("bl", "ch")),
        lambda tensor: lax.all_to_all(
            tensor, ("bl", "ch"), split_axis=3, concat_axis=1, tiled=True
        ),
        lambda tensor: lax.all_to_all(
            tensor, ("bl", "ch"), split_axis=2, concat_axis=3, tiled=True
        ),
        lambda tensor: lax.all_to_all(
            tensor, ("bl", "ch"), split_axis=3, concat_axis=2, tiled=True
        ),
        lambda tensor: lax.all_to_all(
            tensor, ("bl", "ch"), split_axis=1, concat_axis=3, tiled=True
        ),
    )
    grad_field = (gradient * weight[None]).astype(jnp.bfloat16)
    grad_out = lax.psum_scatter(
        jnp.einsum("jr,qcr->jqc", hidden, grad_field, preferred_element_type=jnp.float32),
        "bl",
        scatter_dimension=0,
        tiled=True,
    )
    hidden_grad = jnp.einsum("jqc,qcr->jr", w_out, grad_field, preferred_element_type=jnp.float32)
    grad_in, grad_uvw, grad_base = trunk_grads(
        hidden_grad, pre_act, inputs, w_in, cell_pick, base_pick
    )
    grad_in, grad_uvw, grad_base = lax.psum((grad_in, grad_uvw, grad_base), "ch")
    grad_in, grad_uvw, grad_base = over_rows(grad_in, grad_uvw, grad_base)
    return (grad_out, grad_in, grad_uvw, grad_base)


def solution(mesh):
    return jax.shard_map(
        body,
        mesh=mesh,
        in_specs=(
            P("bl"),
            P("bl"),
            P("bl", "ch"),
            P(),
            P(),
            P(),
            P(None, None, "ch"),
            P(None, "ch", "bl"),
            P(),
        ),
        out_specs=(P("bl", None, "ch"), P(), P(), P()),
        check_vma=False,
    )
```

profile of v0, /device:TPU:1, one launch (start us, length us, event | category | flops | bytes accessed | tf_op | source)
XLA Modules:
  0.0 908.4 jit_solution(5896322105550035754)
XLA Ops:
  7.6 0.9 subtract_bitcast_fusion
  9.2 5.3 copy.101
  14.6 6.5 copy.61
  21.1 2.7 broadcast_multiply_fusion
  24.8 4.1 fusion.1
  28.9 6.7 copy.103
  35.6 11.1 %copy.63 = f32[2,1,32,256,128]{4,2,0,1,3:T(8,128)} copy(f32[2,1,32,256,128]{3,2,4,0,1:T(8,128)} %bitcast.140) | data formatting | bytes 16777216 | tf_op jit(solution)/shard_map/reshape | solution.py:136
  46.6 12.4 %all-to-all-start = ((f32[2,1,32,256,128]{4,2,0,1,3:T(8,128)}), f32[2,1,32,256,128]{4,2,0,1,3:T(8,128)}, u32[]{:S(2)}, u32[]{:S(2)}) async-start(f32[2,1,32,256,128]{4,2,0,1,3:T(8,128)} %copy.63), calls=%async_computation | async-start | bytes 16777216 | tf_op jit(solution)/shard_map/all_to_all | solution.py:143
  59.2 1.1 sine_multiply_fusion
  60.3 101.8 %all-to-all-done = f32[2,1,32,256,128]{4,2,0,1,3:T(8,128)} async-done(((f32[2,1,32,256,128]{4,2,0,1,3:T(8,128)}), f32[2,1,32,256,128]{4,2,0,1,3:T(8,128)}, u32[]{:S(2)}, u32[]{:S(2)}) %all-to-all-start) | async-done | bytes 8388640 | tf_op jit(solution)/shard_map/all_to_all | solution.py:143
  162.1 15.6 %fusion.14 = f32[2,16,256,2,128]{4,2,3,1,0:T(8,128)S(1)} fusion(f32[2,16,8,32,2,128]{5,3,0,4,2,1:T(8,128)} %bitcast.19, f32[1,1,8,32,256]{4,3,0,2,1:T(8,128)S(1)} %get-tuple-element.38, f32[1,1,8,32,256]{4,3,0,2,1:T(8,128)S(1)} %get-tuple-element.37, f32[1,1,8,32,256]{4,3,0,2,1:T(8,128)S(1)} %get-tuple-element.36), kind=kOutput, calls=%fused_computation.21 | convolution fusion | flops 12885688320 | bytes 17563648 | tf_op jit(solution)/shard_map/pacbkr,pqcbt->qatkr/dot_general | solution.py:54
  177.7 1.3 multiply_subtract_fusion.1
  179.1 1.0 pad_maximum_fusion
  180.0 10.1 %copy.66 = f32[2,16,256,2,128]{4,3,1,0,2:T(2,128)} copy(f32[2,16,256,2,128]{4,2,3,1,0:T(8,128)S(1)} %pad_maximum_fusion) | data formatting | bytes 16777216 | tf_op jit(solution)/shard_map/stack | solution.py:41
  190.2 14.3 %all-to-all-start.1 = ((f32[2,16,256,2,128]{4,3,1,0,2:T(2,128)}), f32[2,16,256,2,128]{4,3,1,0,2:T(2,128)}, u32[]{:S(2)}, u32[]{:S(2)}) async-start(f32[2,16,256,2,128]{4,3,1,0,2:T(2,128)} %copy.66), calls=%async_computation.1 | async-start | bytes 16777216 | tf_op jit(solution)/shard_map/all_to_all | solution.py:146
  204.7 1.0 fusion.80
  205.7 1.0 broadcast_multiply_fusion.1
  206.7 1.0 fusion.76
  207.7 1.2 fusion.52
  209.0 98.0 %all-to-all-done.1 = f32[2,16,256,2,128]{4,3,1,0,2:T(2,128)} async-done(((f32[2,16,256,2,128]{4,3,1,0,2:T(2,128)}), f32[2,16,256,2,128]{4,3,1,0,2:T(2,128)}, u32[]{:S(2)}, u32[]{:S(2)}) %all-to-all-start.1) | async-done | bytes 8388640 | tf_op jit(solution)/shard_map/all_to_all | solution.py:146
  307.0 4.5 copy.67
  311.5 1.3 copy.68
  312.9 16.1 %fusion.5 = f32[2,256,16,2,128,1]{4,1,5,0,3,2:T(8,128)S(1)} fusion(f32[2,16,2,256,128,1]{4,1,3,2,0,5:T(8,128)S(1)} %bitcast.138, f32[1,2,256,256]{2,3,0,1:T(8,128)S(1)} %copy-done.3, f32[1,2,256,256]{2,3,0,1:T(8,128)S(1)} %copy-done.4), kind=kOutput, calls=%fused_computation.8 | convolution fusion | flops 12885164032 | bytes 17825792 | tf_op jit(solution)/shard_map/patkr,pqks->qatsr/dot_general | solution.py:62
  329.0 15.5 %fusion.11 = f32[2,16,2,256,128]{4,3,2,1,0:T(8,128)S(1)} fusion(f32[2,256,16,2,128,1]{4,1,5,0,3,2:T(8,128)S(1)} %fusion.5, f32[2,256]{1,0:T(2,128)S(1)} %copy.70, f32[1,2,256,256]{2,3,1,0:T(8,128)S(1)} %get-tuple-element.32, f32[1,2,256,256]{2,3,1,0:T(8,128)S(1)} %get-tuple-element.29), kind=kOutput, calls=%fused_computation.20 | convolution fusion | flops 12887261184 | bytes 17827840 | tf_op jit(solution)/shard_map/patsr,pqsk->qatkr/dot_general | solution.py:69
  344.5 1.3 multiply_subtract_fusion
  345.8 1.0 pad_maximum_fusion.1
  346.8 10.1 %copy.72 = f32[2,16,2,256,128]{4,2,1,0,3:T(2,128)} copy(f32[2,16,2,256,128]{4,3,2,1,0:T(8,128)S(1)} %pad_maximum_fusion.1) | data formatting | bytes 16777216 | tf_op jit(solution)/shard_map/stack | solution.py:41
  356.9 15.7 %all-to-all-start.2 = ((f32[2,16,2,256,128]{4,2,1,0,3:T(2,128)}), f32[2,16,2,256,128]{4,2,1,0,3:T(2,128)}, u32[]{:S(2)}, u32[]{:S(2)}) async-start(f32[2,16,2,256,128]{4,2,1,0,3:T(2,128)} %copy.72), calls=%async_computation.2 | async-start | bytes 16777216 | tf_op jit(solution)/shard_map/all_to_all | solution.py:149
  372.7 1.1 fusion.78
  373.8 101.8 %all-to-all-done.2 = f32[2,16,2,256,128]{4,2,1,0,3:T(2,128)} async-done(((f32[2,16,2,256,128]{4,2,1,0,3:T(2,128)}), f32[2,16,2,256,128]{4,2,1,0,3:T(2,128)}, u32[]{:S(2)}, u32[]{:S(2)}) %all-to-all-start.2) | async-done | bytes 8388640 | tf_op jit(solution)/shard_map/all_to_all | solution.py:149
  475.6 5.7 copy.73
  481.3 14.7 %convolution_bitcast_fusion.1 = f32[2,16,8,32,2,128]{5,3,4,1,2,0:T(8,128)S(1)} fusion(f32[2,16,256,2,128,1,1]{4,2,0,3,1,6,5:T(8,128)S(1)} %bitcast.147, f32[1,1,256,8,32]{2,4,0,3,1:T(8,128)S(1)} %get-tuple-element.35, f32[1,1,256,8,32]{2,4,0,3,1:T(8,128)S(1)} %get-tuple-element.34, f32[1,1,256,8,32]{2,4,0,3,1:T(8,128)S(1)} %get-tuple-element.33), kind=kOutput, calls=%fused_computation.19 | convolution fusion | flops 12885688320 | bytes 17563648 | tf_op jit(solution)/shard_map/patkr,pqtcb->qacbkr/dot_general | solution.py:78
  496.0 1.9 copy.74
  497.9 1.9 copy.75
  499.8 113.6 %all_to_all.66 = f32[2,128,32,2,128]{4,2,3,0,1:T(8,128)S(1)} all-to-all(f32[2,128,32,2,128]{4,2,3,0,1:T(8,128)S(1)} %copy.75), channel_id=1, replica_groups=mesh['bl'=16,'ch'=8] {'bl','ch'}, dimensions={1} | all-to-all | bytes 16777216 | tf_op jit(solution)/shard_map/all_to_all | solution.py:152
  613.5 9.8 %copy.76 = f32[2,1,32,128,2,128]{5,4,3,2,0,1:T(2,128)} copy(f32[2,1,32,128,2,128]{5,2,4,0,3,1:T(8,128)S(1)} %bitcast.143) | data formatting | bytes 16777216 | tf_op jit(solution)/shard_map/all_to_all | solution.py:152
  623.2 8.9 copy.77
  632.1 6.5 fusion.27
  638.8 2.3 fusion.17
  641.1 1.5 fusion.49
  642.7 7.5 fusion.103
  650.2 77.3 %all-reduce.8.cloned.1.call-done = (f32[64,4096]{1,0:T(8,128)}, f32[64,2016]{1,0:T(8,128)}) async-done(((f32[64,4096]{1,0:T(8,128)}, f32[64,2016]{1,0:T(8,128)}), (f32[64,4096]{1,0:T(8,128)}, f32[64,2016]{1,0:T(8,128)})) %all-reduce.8.cloned.1.call-update) | async-done | bytes 1564688 | tf_op jit(solution)/shard_map/psum | solution.py:167
  728.9 30.2 %psum.42 = f32[64,64]{1,0:T(8,128)S(1)} all-reduce(f32[64,64]{1,0:T(8,128)S(1)} %fusion.118), channel_id=1, replica_groups=mesh['bl'=16,'ch'=8] {'ch'}, use_global_device_ids=true, to_apply=%region_1.2 | all-reduce | flops 4096 | bytes 32768 | tf_op jit(solution)/shard_map/psum | solution.py:167
  759.1 68.5 %psum.43 = f32[64,64]{1,0:T(8,128)} all-reduce(f32[64,64]{1,0:T(8,128)S(1)} %psum.42), channel_id=1, replica_groups=mesh['bl'=16,'ch'=8] {'bl'}, use_global_device_ids=true, to_apply=%region_2.3 | all-reduce | flops 4096 | bytes 32768 | tf_op jit(solution)/shard_map/psum | solution.py:95
  827.6 67.5 %all-reduce.6.cloned.1.call-done = (f32[64,2,8192]{2,0,1:T(8,128)}, f32[64,4096]{1,0:T(8,128)}, f32[64,2016]{1,0:T(8,128)}) async-done(((f32[64,2,8192]{2,0,1:T(8,128)}, f32[64,4096]{1,0:T(8,128)}, f32[64,2016]{1,0:T(8,128)}), (f32[64,2,8192]{2,0,1:T(8,128)}, f32[64,4096]{1,0:T(8,128)}, f32[64,2016]{1,0:T(8,128)})) %all-reduce.6.cloned.1.call-update) | async-done | bytes 5758992
  895.1 1.1 constant_dynamic-slice_fusion
  897.1 2.3 copy.129
  899.4 1.9 copy.130
  (51 shorter events, 4.5 us)
Async XLA Ops:
  7.2 17.5 %copy-start = (bf16[64,2,8192]{2,1,0:T(2,128)(2,1)S(1)}, bf16[64,2,8192]{2,1,0:T(2,128)(2,1)}, u32[]{:S(2)}) copy-start(bf16[64,2,8192]{2,1,0:T(2,128)(2,1)} %param.15) | copy-start | bytes 6291460
  21.1 2.8 copy-start.9
  21.1 2.8 copy-start.11
  21.1 3.1 copy-start.10
  21.1 3.1 copy-start.12
  21.1 3.4 copy-start.6
  21.1 3.7 copy-start.2
  23.8 5.1 copy-start.1
  24.4 4.5 copy-start.7
  46.6 115.5 %all-to-all-start = ((f32[2,1,32,256,128]{4,2,0,1,3:T(8,128)}), f32[2,1,32,256,128]{4,2,0,1,3:T(8,128)}, u32[]{:S(2)}, u32[]{:S(2)}) async-start(f32[2,1,32,256,128]{4,2,0,1,3:T(8,128)} %copy.63), calls=%async_computation | async-start | bytes 16777216 | tf_op jit(solution)/shard_map/all_to_all | solution.py:143
  190.2 14.3 %copy-start.5 = (f32[65536]{0:T(1024)S(1)}, f32[65536]{0:T(1024)}, u32[]{:S(2)}) copy-start(f32[65536]{0:T(1024)} %param.17) | copy-start | bytes 786436
  190.2 116.9 %all-to-all-start.1 = ((f32[2,16,256,2,128]{4,3,1,0,2:T(2,128)}), f32[2,16,256,2,128]{4,3,1,0,2:T(2,128)}, u32[]{:S(2)}, u32[]{:S(2)}) async-start(f32[2,16,256,2,128]{4,3,1,0,2:T(2,128)} %copy.66), calls=%async_computation.1 | async-start | bytes 16777216 | tf_op jit(solution)/shard_map/all_to_all | solution.py:146
  311.5 1.4 copy-start.3
  311.5 1.4 copy-start.4
  356.9 118.7 %all-to-all-start.2 = ((f32[2,16,2,256,128]{4,2,1,0,3:T(2,128)}), f32[2,16,2,256,128]{4,2,1,0,3:T(2,128)}, u32[]{:S(2)}, u32[]{:S(2)}) async-start(f32[2,16,2,256,128]{4,2,1,0,3:T(2,128)} %copy.72), calls=%async_computation.2 | async-start | bytes 16777216 | tf_op jit(solution)/shard_map/all_to_all | solution.py:149
  372.6 354.9 %all-reduce.8.cloned.1.call-start = ((), (), s32[]{:S(2)}) async-start(), calls=%async_computation.5 | async-start | bytes 3145728 | tf_op jit(solution)/shard_map/psum | solution.py:167
  642.6 252.5 %all-reduce.6.cloned.1.call-start = ((), (), s32[]{:S(2)}) async-start(), calls=%async_computation.4 | async-start | bytes 11534336
  650.2 77.3 %copy-start.13 = (u32[128]{0:T(128)S(1)}, u32[128]{0:T(128)}, u32[]{:S(2)}) copy-start(u32[128]{0:T(128)} %constant.118) | copy-start | bytes 1540
  650.2 78.6 %copy-start.8 = (bf16[128,64]{0,1:T(8,128)(2,1)S(1)}, bf16[128,64]{0,1:T(8,128)(2,1)}, u32[]{:S(2)}) copy-start(bf16[128,64]{0,1:T(8,128)(2,1)} %copy-done.7) | copy-start | bytes 49156
Sparse Core Ops, SparseCore 0:
  642.8 84.6 all-reduce.7
  730.2 164.8 all-reduce.5
where the time goes:
time: 915 us; the launch traced here: 908 us
  waiting for transfers between devices  446 us (49%)
  blocking collectives  212 us (23%)
  local copies, waits for them, and re-layouts  91.6 us (10%)
  matrix products  84.8 us (9%)
  starting transfers between devices  42.4 us (5%)
  other arithmetic  15.4 us (2%)
  between operations  15.4 us (2%)
    all_to_all x1, blocking collectives, body(): lax.all_to_all(tensor, ('bl', 'ch'), split_axis=1, concat_axis=3, tiled=T...  114 us
    all_to_all x1, waiting for transfers between devices, body(): lax.all_to_all(tensor, ('bl', 'ch'), split_axis=3, concat_axis=2, tiled=T...  102 us
    all_to_all x1, waiting for transfers between devices, body(): lax.all_to_all(tensor, ('bl', 'ch'), split_axis=3, concat_axis=1, tiled=T...  102 us
    all_to_all x1, waiting for transfers between devices, body(): lax.all_to_all(tensor, ('bl', 'ch'), split_axis=2, concat_axis=3, tiled=T...  98 us
    psum x1, waiting for transfers between devices, body(): lax.psum((grad_in, grad_uvw, grad_base), 'ch')  77.3 us
    psum x1, blocking collectives, over_rows(): return lax.psum((grad_in, grad_uvw, grad_base), 'bl')  68.5 us
    unnamed x3, waiting for transfers between devices  67.5 us
    psum x1, blocking collectives, body(): lax.psum((grad_in, grad_uvw, grad_base), 'ch')  30.2 us
  transfers between devices with their start and end apart: 5, of which 5 were waited for; matrix products, arithmetic and copies ran while one was open for 2% of the time, Pallas kernels for 0%

commit v1 on v0

v1 whole, which is shorter than its diff:
```python
import functools
import math

import jax
import jax.numpy as jnp
import ml_dtypes
import numpy as np
from jax import lax
from jax.experimental import pallas as pl
from jax.experimental.pallas import tpu as pltpu
from jax.sharding import PartitionSpec as P

BLOCK = 256
NBLOCKS = 256
CHANNELS = 65536
LOSS_SCALE = 0.0625
HIGHEST = lax.Precision.HIGHEST
F32 = jnp.float32
BF16 = jnp.bfloat16
STEP = 8
WIDE = STEP * BLOCK
LANES = 128
PLANES = 4
VMEM = 56 * 2**20


def split_matrix(matrix):
    high = matrix.astype(ml_dtypes.bfloat16)
    low = (matrix - high.astype(np.float64)).astype(ml_dtypes.bfloat16)
    return high, low


def tables():
    n = np.arange(BLOCK)
    product = np.outer(n, n)
    cosine = np.cos(2 * math.pi * (product % BLOCK) / BLOCK)
    sine = np.sin(2 * math.pi * (product % BLOCK) / BLOCK)
    forward = np.block([[cosine, sine], [-sine, cosine]])
    backward = np.block([[cosine, -sine], [sine, cosine]])
    twiddle = 2 * math.pi * product / CHANNELS
    return (
        *split_matrix(forward),
        *split_matrix(backward),
        np.cos(twiddle).astype(np.float32),
        np.sin(twiddle).astype(np.float32),
    )


def taper_table():
    c = np.arange(CHANNELS)
    window = np.full((CHANNELS,), 0.35875)
    for harmonic, term in ((1, -0.48829), (2, 0.14128), (3, -0.01168)):
        window = window + term * np.cos(2 * math.pi * ((c * harmonic) % CHANNELS) / CHANNELS)
    return window.astype(np.float32).reshape(1, CHANNELS)


def dot(a, b, dims=(((1,), (0,)), ((), ())), precision=None):
    return lax.dot_general(a, b, dims, precision=precision, preferred_element_type=F32)


NT = (((1,), (1,)), ((), ()))
TN = (((0,), (0,)), ((), ()))


def params(**more):
    return pltpu.CompilerParams(vmem_limit_bytes=VMEM, **more)


def one_hot_rows(index_row, count):
    cells = lax.broadcasted_iota(jnp.int32, (count, index_row.shape[1]), 0)
    return jnp.where(cells == index_row, 1.0, 0.0).astype(BF16)


def trunk_kernel(uvw_ref, base_ref, flags_ref, table_ref, features_ref, w_in_ref,
                 inputs_ref, hidden_ref, hidden_t_ref, keep_ref):
    summed = dot(table_ref[...], one_hot_rows(uvw_ref[...], table_ref.shape[1]))
    summed = summed + dot(features_ref[...], one_hot_rows(base_ref[...], features_ref.shape[1]))
    inputs = summed.astype(BF16)
    inputs_ref[...] = inputs.astype(F32)
    pre_act = dot(w_in_ref[...], inputs, TN)
    hidden = pre_act / (1.0 + jnp.exp(-pre_act))
    hidden_ref[...] = hidden.astype(BF16)
    hidden_t_ref[...] = hidden.T.astype(BF16)
    keep_ref[...] = (1.0 - flags_ref[...].astype(F32)).T.astype(BF16)


def trunk(uvw_index, row_baseline, flags, uvw_table, baseline_features, w_in):
    rows = uvw_index.shape[0]
    units = w_in.shape[1]
    return pl.pallas_call(
        trunk_kernel,
        out_shape=(
            jax.ShapeDtypeStruct((w_in.shape[0], rows), F32),
            jax.ShapeDtypeStruct((units, rows), BF16),
            jax.ShapeDtypeStruct((rows, units), BF16),
            jax.ShapeDtypeStruct(flags.shape, BF16),
        ),
        compiler_params=params(),
        name="trunk",
    )(uvw_index[None], row_baseline[None], flags.T, uvw_table, baseline_features, w_in)


def weight_of(keep, taper_row, first_block):
    blocks = keep.shape[1]
    block = lax.broadcasted_iota(jnp.int32, (blocks, WIDE), 0)
    lane = lax.broadcasted_iota(jnp.int32, (blocks, WIDE), 1)
    expand = jnp.where(block == first_block + (lane >> 8), 1.0, 0.0).astype(BF16)
    return dot(keep, expand) * taper_row


def residual_kernel(half, hidden_ref, w_ref, observed_ref, keep_ref, taper_ref, out_ref):
    rows = hidden_ref.shape[0]
    total = observed_ref.shape[2]
    weight = weight_of(keep_ref[...], taper_ref[...], pl.program_id(0) * STEP)
    row = lax.broadcasted_iota(jnp.int32, (rows, total), 0)
    column = lax.broadcasted_iota(jnp.int32, (rows, total), 1)
    pick = jnp.where(column == row + half * rows, -1.0, 0.0).astype(BF16)
    flat = out_ref.reshape(rows * PLANES * STEP, LANES)
    for q in range(2):
        residual = dot(hidden_ref[...], w_ref[q]) + dot(pick, observed_ref[q], NT)
        residual = residual * weight
        for b in range(STEP):
            for side in range(2):
                start = b * BLOCK + side * LANES
                flat[pl.ds((q * 2 + side) * STEP + b, rows, stride=PLANES * STEP), :] = residual[
                    :, start : start + LANES
                ]


def residual_part(half, halves, hidden_t, w, observed, keep, taper):
    rows = hidden_t.shape[0] // halves
    blocks = keep.shape[1]
    return pl.pallas_call(
        functools.partial(residual_kernel, half),
        grid=(blocks // STEP,),
        in_specs=[
            pl.BlockSpec((rows, hidden_t.shape[1]), lambda g: (half, 0)),
            pl.BlockSpec((2, w.shape[1], WIDE), lambda g: (0, 0, g)),
            pl.BlockSpec((2, WIDE, observed.shape[2]), lambda g: (0, g, 0)),
            pl.BlockSpec((rows, blocks), lambda g: (half, 0)),
            pl.BlockSpec((1, WIDE), lambda g: (0, g)),
        ],
        out_specs=pl.BlockSpec((rows, PLANES, STEP, LANES), lambda g: (0, 0, g, 0)),
        out_shape=jax.ShapeDtypeStruct((rows, PLANES, blocks, LANES), F32),
        compiler_params=params(),
        cost_estimate=pl.CostEstimate(
            flops=2 * rows * 2 * blocks * BLOCK * 192, bytes_accessed=10 * 2**20, transcendentals=0
        ),
        name=f"residual_{half}",
    )(hidden_t, w, observed, keep, taper)


def halves_of(values):
    high = values.astype(BF16)
    return high, (values - high.astype(F32)).astype(BF16)


def dot_three(a, b):
    return dot(a[0], b[0]) + (dot(a[0], b[1]) + dot(a[1], b[0]))


def delay_kernel(pieces, x_ref, fh_ref, fl_ref, bh_ref, bl_ref, cos_ref, sin_ref, weight_ref, *outs):
    forward = (fh_ref[...], fl_ref[...])
    backward = (bh_ref[...], bl_ref[...])
    cosine, sine = cos_ref[...], sin_ref[...]
    count = x_ref.shape[1]
    members, local = x_ref.shape[0], x_ref.shape[3]
    turned = []
    for i in range(count):
        values = jnp.concatenate(
            [
                jnp.concatenate(
                    [x_ref[:, i, q * 2 + side].reshape(NBLOCKS, LANES) for side in range(2)], axis=1
                )
                for q in range(2)
            ],
            axis=0,
        )
        first = dot_three(forward, halves_of(values))
        real, imag = first[:NBLOCKS], first[NBLOCKS:]
        turned.append(
            jnp.concatenate([real * cosine + imag * sine, imag * cosine - real * sine], axis=1)
        )
    second = dot_three(halves_of(jnp.concatenate(turned, axis=0)), backward)
    factor = weight_ref[...] * (LOSS_SCALE / CHANNELS)
    factor = jnp.concatenate([jnp.concatenate([factor, factor], axis=1)] * count, axis=0)
    third = dot_three(halves_of(second * factor), forward)
    for i in range(count):
        part = third[i * NBLOCKS : (i + 1) * NBLOCKS]
        real, imag = part[:, :BLOCK], part[:, BLOCK:]
        back = jnp.concatenate([real * cosine - imag * sine, imag * cosine + real * sine], axis=0)
        fourth = dot_three(backward, halves_of(back))
        for q in range(2):
            for member in range(members):
                start = q * NBLOCKS + member * local
                for out_ref, size in zip(outs, pieces):
                    for side in range(2):
                        out_ref[member, i, q * 2 + side] = fourth[
                            start : start + size, side * LANES : (side + 1) * LANES
                        ]
                    start += size


def delay_filter(pieces, arrived, constants, weight, count=2):
    members, rows, _, local, _ = arrived.shape
    whole = lambda array: pl.BlockSpec(array.shape, lambda g: (0, 0))
    flops = rows * 4 * 3 * 2 * 512 * 512 * 256
    return pl.pallas_call(
        functools.partial(delay_kernel, pieces),
        grid=(rows // count,),
        in_specs=[
            pl.BlockSpec((members, count, PLANES, local, LANES), lambda g: (0, g, 0, 0, 0)),
            *[whole(array) for array in constants],
            whole(weight),
        ],
        out_specs=[
            pl.BlockSpec((members, count, PLANES, size, LANES), lambda g: (0, g, 0, 0, 0))
            for size in pieces
        ],
        out_shape=[
            jax.ShapeDtypeStruct((members, rows, PLANES, size, LANES), F32) for size in pieces
        ],
        compiler_params=params(),
        cost_estimate=pl.CostEstimate(flops=flops, bytes_accessed=12 * 2**20, transcendentals=0),
        name=f"delay_{len(pieces)}",
    )(arrived, *constants, weight)


def tail_kernel(first, g1_ref, g2_ref, hidden_ref, w_ref, keep_ref, taper_ref,
                mine_ref, other_ref, hidden_grad_ref):
    step = pl.program_id(0)
    weight = weight_of(keep_ref[...], taper_ref[...], (first + step) * STEP)
    rows = g1_ref.shape[0]
    flats = [ref.reshape(rows * PLANES * STEP, LANES) for ref in (g1_ref, g2_ref)]

    @pl.when(step == 0)
    def _():
        hidden_grad_ref[...] = jnp.zeros_like(hidden_grad_ref)

    total = hidden_grad_ref[...]
    for q in range(2):
        values = jnp.concatenate(
            [
                jnp.concatenate(
                    [
                        flat[pl.ds((q * 2 + side) * STEP + b, rows, stride=PLANES * STEP), :]
                        for b in range(STEP)
                        for side in range(2)
                    ],
                    axis=1,
                )
                for flat in flats
            ],
            axis=0,
        )
        grad_field = (values * weight).astype(BF16)
        grad_out = dot(hidden_ref[...], grad_field)
        units = grad_out.shape[0] // 2
        for d in range(4):
            mine_ref[d, q] = grad_out[d * 8 : (d + 1) * 8]
            other_ref[d, q] = grad_out[units + d * 8 : units + (d + 1) * 8]
        total = total + dot(w_ref[q], grad_field, NT)
    hidden_grad_ref[...] = total


def tail_part(first, count, g1, g2, hidden_order, w, keep, taper):
    rows = g1.shape[0]
    units, total_rows = hidden_order.shape
    return pl.pallas_call(
        functools.partial(tail_kernel, first),
        grid=(count,),
        in_specs=[
            pl.BlockSpec((rows, PLANES, STEP, LANES), lambda g: (0, 0, first + g, 0)),
            pl.BlockSpec((rows, PLANES, STEP, LANES), lambda g: (0, 0, g, 0)),
            pl.BlockSpec((units, total_rows), lambda g: (0, 0)),
            pl.BlockSpec((2, units, WIDE), lambda g: (0, 0, first + g)),
            pl.BlockSpec(keep.shape, lambda g: (0, 0)),
            pl.BlockSpec((1, WIDE), lambda g: (0, first + g)),
        ],
        out_specs=[
            pl.BlockSpec((4, 2, 8, WIDE), lambda g: (0, 0, 0, g)),
            pl.BlockSpec((4, 2, 8, WIDE), lambda g: (0, 0, 0, g)),
            pl.BlockSpec((units, total_rows), lambda g: (0, 0)),
        ],
        out_shape=[
            jax.ShapeDtypeStruct((4, 2, 8, count * WIDE), F32),
            jax.ShapeDtypeStruct((4, 2, 8, count * WIDE), F32),
            jax.ShapeDtypeStruct((units, total_rows), F32),
        ],
        compiler_params=params(),
        cost_estimate=pl.CostEstimate(
            flops=count * 2 * 2 * 2 * 64 * 128 * WIDE, bytes_accessed=count * 4 * 2**20, transcendentals=0
        ),
        name=f"tail_{first}",
    )(g1, g2, hidden_order, w, keep, taper)


def terms_of(values, count):
    out = []
    for _ in range(count):
        term = values.astype(BF16)
        out.append(term)
        values = values - term.astype(F32)
    return out


def scatter_kernel(hidden_grad_ref, inputs_ref, index_ref, w_in_ref, w_in_t_ref,
                   grad_in_ref, grad_uvw_ref, grad_base_ref, terms_ref):
    inputs = inputs_ref[...].astype(BF16)
    pre_act = dot(w_in_t_ref[...], inputs)
    sigmoid = 1.0 / (1.0 + jnp.exp(-pre_act))
    pre_grad = hidden_grad_ref[...] * sigmoid * (1.0 + pre_act * (1.0 - sigmoid))
    grad_terms = jnp.concatenate(terms_of(pre_grad, 3), axis=0)
    units = pre_grad.shape[0]
    parts = dot(inputs, grad_terms, NT)
    grad_in_ref[...] = parts[:, :units] + (parts[:, units : 2 * units] + parts[:, 2 * units :])
    input_grad = jnp.zeros_like(pre_grad)
    for k in (2, 1, 0):
        input_grad = input_grad + dot(w_in_ref[...], grad_terms[k * units : (k + 1) * units])
    terms_ref[...] = jnp.concatenate(terms_of(input_grad, 3), axis=0)
    for which, out_ref in ((0, grad_uvw_ref), (1, grad_base_ref)):
        index = index_ref[which : which + 1, :].astype(jnp.int32)
        cells = out_ref.shape[1]
        for start in range(0, cells, 512):
            size = min(512, cells - start)
            picked = one_hot_rows(index - start, size)
            sums = dot(terms_ref[...], picked, NT)
            out_ref[:, start : start + size] = sums[:units] + (
                sums[units : 2 * units] + sums[2 * units :]
            )


def scatter(hidden_grad, inputs, index, w_in, cells, baselines):
    units, rows = hidden_grad.shape
    return pl.pallas_call(
        scatter_kernel,
        out_shape=[
            jax.ShapeDtypeStruct(w_in.shape, F32),
            jax.ShapeDtypeStruct((w_in.shape[0], cells), F32),
            jax.ShapeDtypeStruct((w_in.shape[0], baselines), F32),
        ],
        scratch_shapes=[pltpu.VMEM((3 * units, rows), BF16)],
        compiler_params=params(),
        name="scatter",
    )(hidden_grad, inputs, index, w_in, w_in.T)


def swap(values, axis, distance):
    size = lax.axis_size(axis)
    return lax.ppermute(values, axis, [(i, i ^ distance) for i in range(size)])


def gather_rows(values):
    me = lax.axis_index("bl")
    values = values[None]
    for distance in (8, 4, 2, 1):
        got = swap(values, "bl", distance)
        mine_first = (me & distance) == 0
        low = jnp.where(mine_first, values, got)
        high = jnp.where(mine_first, got, values)
        values = jnp.stack([low, high], axis=1).reshape(-1, *values.shape[1:])
    members, height, width = values.shape
    return values.transpose(1, 0, 2).reshape(height, members * width)


def sum_over_rows(mine, other):
    ring = lambda d: [(i, (i + 4 * d) % 16) for i in range(16)]
    both = mine + swap(other, "bl", 1)
    got = [lax.ppermute(both[d], "bl", ring(d)) for d in (1, 2, 3)]
    total = both[0] + got[0] + got[1] + got[2]
    return total[:, :4] + swap(total[:, 4:], "bl", 2)


def body(
    uvw_index, row_baseline, flags, uvw_table, baseline_features, w_in, w_out, observed, delay_weight
):
    members = lax.axis_size("ch")
    rows = uvw_index.shape[0]
    local_blocks = flags.shape[1]
    local_channels = w_out.shape[2]
    half_rows = rows // 2
    per = half_rows // members

    inputs, hidden, hidden_t, keep = trunk(
        uvw_index, row_baseline, flags, uvw_table, baseline_features, w_in
    )
    w = w_out.transpose(1, 0, 2)
    taper = lax.dynamic_slice_in_dim(
        jnp.asarray(taper_table()), lax.axis_index("ch") * local_channels, local_channels, 1
    )
    constants = [jnp.asarray(table) for table in tables()]
    weight = delay_weight.reshape(BLOCK, NBLOCKS).T

    def exchange(values):
        size = values.shape[-2]
        got = lax.all_to_all(
            values.reshape(members, per, PLANES, size, LANES), "ch", 0, 0, tiled=True
        )
        return got

    sent = [
        exchange(residual_part(half, 2, hidden_t, w, observed, keep, taper)) for half in range(2)
    ]
    (out_0,) = delay_filter((local_blocks,), sent[0], constants, weight)
    back_0 = exchange(out_0).reshape(half_rows, PLANES, local_blocks, LANES)
    pieces = (local_blocks // 2, local_blocks // 2)
    back_1 = [
        exchange(out).reshape(half_rows, PLANES, size, LANES)
        for out, size in zip(delay_filter(pieces, sent[1], constants, weight), pieces)
    ]

    me = lax.axis_index("bl")
    order = lax.broadcasted_iota(jnp.int32, hidden.shape[:1], 0)
    core, x_far, y_far, unit = order // 32, (order // 8) % 4, (order // 4) % 2, order % 4
    owner = ((me // 4 + x_far) % 4) * 4 + ((me // 2) % 2 ^ y_far) * 2 + (me % 2 ^ core)
    units = lax.broadcasted_iota(jnp.int32, (hidden.shape[0],) * 2, 1)
    turn = (units == (owner * 4 + unit)[:, None]).astype(BF16)
    hidden_order = dot(turn, hidden).astype(BF16)

    index_rows = jnp.stack([uvw_index, row_baseline]).astype(F32)
    early = jnp.concatenate([inputs, index_rows, jnp.zeros((6, rows), F32)], axis=0)
    early = gather_rows(early)

    first = 0
    grad_out = []
    hidden_grad = 0.0
    for piece, size in zip(back_1, pieces):
        count = size // STEP
        mine, other, grad = tail_part(
            first, count, back_0, piece, hidden_order, w, keep, taper
        )
        hidden_grad = hidden_grad + grad
        grad_out.append(sum_over_rows(mine, other))
        first += count
    grad_out = jnp.concatenate(grad_out, axis=2).transpose(1, 0, 2)

    for distance in (1, 2, 4):
        hidden_grad = hidden_grad + swap(hidden_grad, "ch", distance)
    hidden_grad = gather_rows(hidden_grad)
    inputs_all, index_all = early[: w_in.shape[0]], early[w_in.shape[0] :]
    grad_in, grad_uvw, grad_base = scatter(
        hidden_grad, inputs_all, index_all, w_in, uvw_table.shape[1], baseline_features.shape[1]
    )
    return (grad_out, grad_in, grad_uvw, grad_base)


def solution(mesh):
    return jax.shard_map(
        body,
        mesh=mesh,
        in_specs=(
            P("bl"),
            P("bl"),
            P("bl", "ch"),
            P(),
            P(),
            P(),
            P(None, None, "ch"),
            P(None, "ch", "bl"),
            P(),
        ),
        out_specs=(P("bl", None, "ch"), P(), P(), P()),
        check_vma=False,
    )
```

time: 915 us -> 327 us (0.36)
  waiting for transfers between devices: 446 us -> 116 us
  blocking collectives: 212 us -> 52.2 us
  matrix products: 84.8 us -> 0.79 us
  local copies, waits for them, and re-layouts: 91.6 us -> 11.5 us
  Pallas kernels: 0 us -> 77.7 us
  starting transfers between devices: 42.4 us -> 64.5 us
  between operations: 15.4 us -> 0.98 us
  other arithmetic: 15.4 us -> 1.85 us
    all_to_all x3 -> x4, waiting for transfers between devices: 302 us -> 87.6 us  [exchange(): lax.all_to_all(values.reshape(members, per, PLANES, size, LANES), 'ch', 0...]
    psum x2 -> x0, blocking collectives: 98.7 us -> none  [the longest x1 68.5 us: over_rows(): return lax.psum((grad_in, grad_uvw, grad_base), 'bl')]
    dot_general x14 -> x1, matrix products: 84.8 us -> 0.79 us  [dot(): lax.dot_general(a, b, dims, precision=precision, preferred_element_type=F32)]
    pallas_call x0 -> x8, Pallas kernels: none -> 77.7 us  [the longest x2 36 us: delay_filter(): pl.pallas_call(functools.partial(delay_kernel, pieces), grid=(rows // cou...]
    psum x1 -> x0, waiting for transfers between devices: 77.3 us -> none  [body(): lax.psum((grad_in, grad_uvw, grad_base), 'ch')]
    unnamed x3 -> x0, waiting for transfers between devices: 67.5 us -> none
    all_to_all x1, blocking collectives: 114 us -> 52.2 us  [exchange(): lax.all_to_all(values.reshape(members, per, PLANES, size, LANES), 'ch', 0...]
    ppermute x0 -> x21, starting transfers between devices: none -> 44.5 us  [the longest x15 37.4 us: swap(): return lax.ppermute(values, axis, [(i, i ^ distance) for i in range(size)])]
  transfers between devices with their start and end apart: 5 -> 25, of which waited for: 5 -> 14; matrix products, arithmetic and copies ran while one was open for 2% -> 2% of each run, Pallas kernels for 0% -> 21%
where the time goes in v1:
time: 327 us; the launch traced here: 326 us
  waiting for transfers between devices  116 us (35%)
  Pallas kernels  77.7 us (24%)
  starting transfers between devices  64.5 us (20%)
  blocking collectives  52.2 us (16%)
  local copies, waits for them, and re-layouts  11.5 us (4%)
    all_to_all x4, waiting for transfers between devices, exchange(): lax.all_to_all(values.reshape(members, per, PLANES, size, LANES), 'ch', 0...  87.6 us
    all_to_all x1, blocking collectives, exchange(): lax.all_to_all(values.reshape(members, per, PLANES, size, LANES), 'ch', 0...  52.2 us
    ppermute x15, starting transfers between devices, swap(): return lax.ppermute(values, axis, [(i, i ^ distance) for i in range(size)])  37.4 us
    pallas_call x2, Pallas kernels, delay_filter(): pl.pallas_call(functools.partial(delay_kernel, pieces), grid=(rows // cou...  36 us
    all_to_all x4, starting transfers between devices, exchange(): lax.all_to_all(values.reshape(members, per, PLANES, size, LANES), 'ch', 0...  20 us
    ppermute x6, waiting for transfers between devices, sum_over_rows(): got = [lax.ppermute(both[d], 'bl', ring(d)) for d in (1, 2, 3)]  19.1 us
    pallas_call x2, Pallas kernels, residual_part(): pl.pallas_call(functools.partial(residual_kernel, half), grid=(blocks //...  16.2 us
    pallas_call x2, Pallas kernels, tail_part(): pl.pallas_call(functools.partial(tail_kernel, first), grid=(count,), in_s...  13.2 us
  transfers between devices with their start and end apart: 25, of which 14 were waited for; matrix products, arithmetic and copies ran while one was open for 2% of the time, Pallas kernels for 21%

profile of v1, /device:TPU:1, one launch (start us, length us, event | category | flops | bytes accessed | tf_op | source)
XLA Modules:
  0.0 325.8 jit_solution(17056212046664542225)
XLA Ops:
  0.6 4.1 %copy.63 = bf16[64,2,8192]{2,0,1:T(8,128)(2,1)} copy(bf16[64,2,8192]{2,1,0:T(2,128)(2,1)} %param.22) | data formatting | bytes 4194304 | tf_op args[6]
  4.7 1.4 constant_dynamic-slice_fusion.taper_ref
  6.1 2.5 trunk.1
  8.6 8.1 %residual_1.1 = f32[64,4,32,128]{3,2,1,0:T(8,128)} custom-call(bf16[128,64]{1,0:T(8,128)(2,1)} %get-tuple-element.19.hidden_ref, bf16[2,64,8192]{2,1,0:T(8,128)(2,1)} %bitcast.124, bf16[2,8192,128]{2,1,0:T(8,128)(2,1)} %observed_ref.3, bf16[128,32]{1,0:T(8,128)(2,1)} %get-tuple-element.20.keep_ref, f32[1,8192]{1,0:T(1,128)} %constant_dynamic-slice_fusion.taper_ref), custom_call_target="tpu_custom_call" | custom-call | flops 402653184 | bytes 10485760 | tf_op jit(solution)/shard_map/residual_1/pallas_call | solution.py:133
  16.7 6.9 %all-to-all-start.2 = ((f32[8,8,4,32,128]{4,3,2,1,0:T(8,128)}), f32[8,8,4,32,128]{4,3,2,1,0:T(8,128)}, u32[]{:S(2)}, u32[]{:S(2)}) async-start(f32[8,8,4,32,128]{4,3,2,1,0:T(8,128)} %bitcast.131), calls=%async_computation.2 | async-start | bytes 8388608 | tf_op jit(solution)/shard_map/all_to_all | solution.py:396
  23.6 8.1 %residual_0.1 = f32[64,4,32,128]{3,2,1,0:T(8,128)} custom-call(bf16[128,64]{1,0:T(8,128)(2,1)} %get-tuple-element.19.hidden_ref, bf16[2,64,8192]{2,1,0:T(8,128)(2,1)} %bitcast.125, bf16[2,8192,128]{2,1,0:T(8,128)(2,1)} %observed_ref.3, bf16[128,32]{1,0:T(8,128)(2,1)} %get-tuple-element.20.keep_ref, f32[1,8192]{1,0:T(1,128)} %constant_dynamic-slice_fusion.taper_ref), custom_call_target="tpu_custom_call" | custom-call | flops 402653184 | bytes 10485760 | tf_op jit(solution)/shard_map/residual_0/pallas_call | solution.py:133
  31.7 40.5 %all-to-all-done.2.x_ref = f32[8,8,4,32,128]{4,3,2,1,0:T(8,128)} async-done(((f32[8,8,4,32,128]{4,3,2,1,0:T(8,128)}), f32[8,8,4,32,128]{4,3,2,1,0:T(8,128)}, u32[]{:S(2)}, u32[]{:S(2)}) %all-to-all-start.2) | async-done | bytes 4194336 | tf_op jit(solution)/shard_map/all_to_all | solution.py:396
  72.3 4.7 %all-to-all-start = ((f32[8,8,4,32,128]{4,3,2,1,0:T(8,128)}), f32[8,8,4,32,128]{4,3,2,1,0:T(8,128)}, u32[]{:S(2)}, u32[]{:S(2)}) async-start(f32[8,8,4,32,128]{4,3,2,1,0:T(8,128)} %bitcast.130), calls=%async_computation | async-start | bytes 8388608 | tf_op jit(solution)/shard_map/all_to_all | solution.py:396
  77.0 0.8 copy.47
  77.9 18.0 %delay_2.1 = (f32[8,8,4,16,128]{4,3,2,1,0:T(8,128)}, f32[8,8,4,16,128]{4,3,2,1,0:T(8,128)}) custom-call(f32[8,8,4,32,128]{4,3,2,1,0:T(8,128)} %all-to-all-done.2.x_ref, bf16[512,512]{1,0:T(8,128)(2,1)} %constant.137.clone.fh_ref, bf16[512,512]{1,0:T(8,128)(2,1)} %constant.138.clone.fl_ref, bf16[512,512]{1,0:T(8,128)(2,1)} %constant.139.clone.bh_ref, ...), custom_call_target="tpu_custom_call" | custom-call | flops 12884901888 | bytes 12582912 | tf_op jit(solution)/shard_map/delay_2/pallas_call | solution.py:208
  95.8 28.7 %all-to-all-done.x_ref = f32[8,8,4,32,128]{4,3,2,1,0:T(8,128)} async-done(((f32[8,8,4,32,128]{4,3,2,1,0:T(8,128)}), f32[8,8,4,32,128]{4,3,2,1,0:T(8,128)}, u32[]{:S(2)}, u32[]{:S(2)}) %all-to-all-start) | async-done | bytes 4194336 | tf_op jit(solution)/shard_map/all_to_all | solution.py:396
  124.6 4.7 %all-to-all-start.4 = ((f32[8,8,4,16,128]{4,3,2,1,0:T(8,128)}), f32[8,8,4,16,128]{4,3,2,1,0:T(8,128)S(1)}, u32[]{:S(2)}, u32[]{:S(2)}) async-start(f32[8,8,4,16,128]{4,3,2,1,0:T(8,128)} %get-tuple-element.25), calls=%async_computation.4 | async-start | bytes 4194304 | tf_op jit(solution)/shard_map/all_to_all | solution.py:396
  129.3 18.0 %delay_1.1 = f32[8,8,4,32,128]{4,3,2,1,0:T(8,128)} custom-call(f32[8,8,4,32,128]{4,3,2,1,0:T(8,128)} %all-to-all-done.x_ref, bf16[512,512]{1,0:T(8,128)(2,1)} %constant.137.clone.fh_ref, bf16[512,512]{1,0:T(8,128)(2,1)} %constant.138.clone.fl_ref, bf16[512,512]{1,0:T(8,128)(2,1)} %constant.139.clone.bh_ref, bf16[512,512]{1,0:T(8,128)(2,1)} %constant.140.clone.bl_ref, ...), custom_call_target="tpu_custom_call" | custom-call | flops 12884901888 | bytes 12582912 | tf_op jit(solution)/shard_map/delay_1/pallas_call | solution.py:208
  147.3 7.3 %all-to-all-done.4 = f32[8,8,4,16,128]{4,3,2,1,0:T(8,128)S(1)} async-done(((f32[8,8,4,16,128]{4,3,2,1,0:T(8,128)}), f32[8,8,4,16,128]{4,3,2,1,0:T(8,128)S(1)}, u32[]{:S(2)}, u32[]{:S(2)}) %all-to-all-start.4) | async-done | bytes 2097184 | tf_op jit(solution)/shard_map/all_to_all | solution.py:396
  154.6 52.2 %all_to_all.25 = f32[8,8,4,32,128]{4,3,2,1,0:T(8,128)} all-to-all(f32[8,8,4,32,128]{4,3,2,1,0:T(8,128)} %delay_1.1), channel_id=1, replica_groups=mesh['bl'=16,'ch'=8] {'ch'}, dimensions={0} | all-to-all | bytes 8388608 | tf_op jit(solution)/shard_map/all_to_all | solution.py:396
  206.8 3.7 %all-to-all-start.3 = ((f32[8,8,4,16,128]{4,3,2,1,0:T(8,128)}), f32[8,8,4,16,128]{4,3,2,1,0:T(8,128)S(1)}, u32[]{:S(2)}, u32[]{:S(2)}) async-start(f32[8,8,4,16,128]{4,3,2,1,0:T(8,128)} %get-tuple-element.21), calls=%async_computation.3 | async-start | bytes 4194304 | tf_op jit(solution)/shard_map/all_to_all | solution.py:396
  210.8 2.7 collective-permute-start.17
  215.2 1.4 collective-permute-start.18
  216.6 6.6 %tail_2.1 = (f32[4,2,8,4096]{3,2,1,0:T(8,128)}, f32[4,2,8,4096]{3,2,1,0:T(8,128)}, f32[64,128]{1,0:T(8,128)}) custom-call(f32[64,4,32,128]{3,2,1,0:T(8,128)} %bitcast.128, f32[64,4,16,128]{3,2,1,0:T(8,128)} %bitcast.132, bf16[64,128]{1,0:T(8,128)(2,1)} %convolution_convert_fusion.hidden_ref, bf16[2,64,8192]{2,1,0:T(8,128)(2,1)} %bitcast.126, ...), custom_call_target="tpu_custom_call" | custom-call | flops 268435456 | bytes 8388608 | tf_op jit(solution)/shard_map/tail_2/pallas_call | solution.py:269
  223.2 11.0 %all-to-all-done.3 = f32[8,8,4,16,128]{4,3,2,1,0:T(8,128)S(1)} async-done(((f32[8,8,4,16,128]{4,3,2,1,0:T(8,128)}), f32[8,8,4,16,128]{4,3,2,1,0:T(8,128)S(1)}, u32[]{:S(2)}, u32[]{:S(2)}) %all-to-all-start.3) | async-done | bytes 2097184 | tf_op jit(solution)/shard_map/all_to_all | solution.py:396
  234.2 1.4 copy-done.1
  235.5 6.6 %tail_0.1 = (f32[4,2,8,4096]{3,2,1,0:T(8,128)}, f32[4,2,8,4096]{3,2,1,0:T(8,128)}, f32[64,128]{1,0:T(8,128)}) custom-call(f32[64,4,32,128]{3,2,1,0:T(8,128)} %bitcast.129, f32[64,4,16,128]{3,2,1,0:T(8,128)} %bitcast.133, bf16[64,128]{1,0:T(8,128)(2,1)} %convolution_convert_fusion.hidden_ref, bf16[2,64,8192]{2,1,0:T(8,128)(2,1)} %bitcast.127, ...), custom_call_target="tpu_custom_call" | custom-call | flops 268435456 | bytes 8388608 | tf_op jit(solution)/shard_map/tail_0/pallas_call | solution.py:269
  242.2 0.9 add.156
  243.8 2.0 collective-permute-done.10
  245.8 2.1 collective-permute-start.11
  248.0 1.3 collective-permute-done.11
  249.2 2.1 collective-permute-start.12
  251.3 2.8 collective-permute-start.19
  254.1 2.8 collective-permute-start.13
  256.9 1.5 collective-permute-done.13
  258.5 1.3 collective-permute-start.14
  259.8 7.8 %collective-permute-start.20 = (f32[8,72,128]{2,1,0:T(8,128)S(1)}, f32[8,72,128]{2,1,0:T(8,128)S(1)}, u32[]{:S(2)}, u32[]{:S(2)}) collective-permute-start(f32[8,72,128]{2,1,0:T(8,128)S(1)} %bitcast.137), channel_id=1, source_target_pairs={{0,8},{8,0},{16,24},{24,16},{32,40},{40,32},{48,56},{56,48},{64,72... | collective-permute-start | bytes 884744 | tf_op jit(solution)/shard_map/ppermute | solution.py:350
  267.7 2.8 collective-permute-start.15
  270.7 3.0 collective-permute-start.5
  273.8 3.3 %collective-permute-start.16 = (f32[8,64,128]{2,1,0:T(8,128)S(1)}, f32[8,64,128]{2,1,0:T(8,128)S(1)}, u32[]{:S(2)}, u32[]{:S(2)}) collective-permute-start(f32[8,64,128]{2,1,0:T(8,128)S(1)} %bitcast.138), channel_id=1, source_target_pairs={{0,8},{8,0},{16,24},{24,16},{32,40},{40,32},{48,56},{56,48},{64,72... | collective-permute-start | bytes 786440 | tf_op jit(solution)/shard_map/ppermute | solution.py:350
  278.5 1.1 copy_bitcast_fusion.1
  279.6 9.8 %scatter.1 = (f32[64,64]{1,0:T(8,128)}, f32[64,4096]{1,0:T(8,128)}, f32[64,2016]{1,0:T(8,128)}) custom-call(f32[64,2048]{1,0:T(8,128)} %get-tuple-element.73.hidden_grad_ref, f32[64,2048]{1,0:T(8,128)} %get-tuple-element.72.inputs_ref, f32[8,2048]{1,0:T(8,128)} %slice_bitcast_fusion.9.index_ref, bf16[64,64]{1,0:T(8,128)(2,1)} %w_in_ref.3, ...), custom_call_target="tpu_custom_call" | custom-call | tf_op jit(solution)/shard_map/scatter/pallas_call | solution.py:335
  289.5 2.6 collective-permute-start.8
  293.3 2.1 collective-permute-start.3
  295.5 1.3 collective-permute-start.2
  296.8 5.4 %collective-permute-done.8 = f32[2,8,4096]{2,1,0:T(8,128)S(1)} collective-permute-done((f32[2,8,4096]{2,1,0:T(8,128)S(1)}, f32[2,8,4096]{2,1,0:T(8,128)S(1)}, u32[]{:S(2)}, u32[]{:S(2)}) %collective-permute-start.8) | collective-permute-done | bytes 262176 | tf_op jit(solution)/shard_map/ppermute | solution.py:369
  302.3 6.2 %collective-permute-done.6 = f32[2,8,4096]{2,1,0:T(8,128)S(1)} collective-permute-done((f32[2,8,4096]{2,1,0:T(8,128)S(1)}, f32[2,8,4096]{2,1,0:T(8,128)S(1)}, u32[]{:S(2)}, u32[]{:S(2)}) %collective-permute-start.6) | collective-permute-done | bytes 262176 | tf_op jit(solution)/shard_map/ppermute | solution.py:369
  308.6 2.6 collective-permute-start.9
  311.2 3.0 collective-permute-done.3
  314.2 4.4 %collective-permute-done.1 = f32[2,8,4096]{2,1,0:T(8,128)S(1)} collective-permute-done((f32[2,8,4096]{2,1,0:T(8,128)S(1)}, f32[2,8,4096]{2,1,0:T(8,128)S(1)}, u32[]{:S(2)}, u32[]{:S(2)}) %collective-permute-start.1) | collective-permute-done | bytes 262176 | tf_op jit(solution)/shard_map/ppermute | solution.py:369
  318.7 2.6 collective-permute-start.4
  321.4 3.4 %collective-permute-done.4 = f32[2,4,4096]{2,1,0:T(4,128)S(1)} collective-permute-done((f32[2,4,4096]{2,1,0:T(4,128)S(1)}, f32[2,4,4096]{2,1,0:T(4,128)S(1)}, u32[]{:S(2)}, u32[]{:S(2)}) %collective-permute-start.4) | collective-permute-done | bytes 131104 | tf_op jit(solution)/shard_map/ppermute | solution.py:350
  324.9 0.9 copy.57
  (88 shorter events, 6.1 us)
Async XLA Ops:
  16.7 55.5 %all-to-all-start.2 = ((f32[8,8,4,32,128]{4,3,2,1,0:T(8,128)}), f32[8,8,4,32,128]{4,3,2,1,0:T(8,128)}, u32[]{:S(2)}, u32[]{:S(2)}) async-start(f32[8,8,4,32,128]{4,3,2,1,0:T(8,128)} %bitcast.131), calls=%async_computation.2 | async-start | bytes 8388608 | tf_op jit(solution)/shard_map/all_to_all | solution.py:396
  72.2 4.7 %copy-start.4 = (f32[65536]{0:T(1024)S(1)}, f32[65536]{0:T(1024)}, u32[]{:S(2)}) copy-start(f32[65536]{0:T(1024)} %param.24) | copy-start | bytes 786436
  72.3 52.3 %all-to-all-start = ((f32[8,8,4,32,128]{4,3,2,1,0:T(8,128)}), f32[8,8,4,32,128]{4,3,2,1,0:T(8,128)}, u32[]{:S(2)}, u32[]{:S(2)}) async-start(f32[8,8,4,32,128]{4,3,2,1,0:T(8,128)} %bitcast.130), calls=%async_computation | async-start | bytes 8388608 | tf_op jit(solution)/shard_map/all_to_all | solution.py:396
  124.6 30.0 %all-to-all-start.4 = ((f32[8,8,4,16,128]{4,3,2,1,0:T(8,128)}), f32[8,8,4,16,128]{4,3,2,1,0:T(8,128)S(1)}, u32[]{:S(2)}, u32[]{:S(2)}) async-start(f32[8,8,4,16,128]{4,3,2,1,0:T(8,128)} %get-tuple-element.25), calls=%async_computation.4 | async-start | bytes 4194304 | tf_op jit(solution)/shard_map/all_to_all | solution.py:396
  154.6 52.2 %copy-start = (f32[8,8,4,16,128]{4,3,2,1,0:T(8,128)}, f32[8,8,4,16,128]{4,3,2,1,0:T(8,128)S(1)}, u32[]{:S(2)}) copy-start(f32[8,8,4,16,128]{4,3,2,1,0:T(8,128)S(1)} %all-to-all-done.4) | copy-start | bytes 6291460
  206.8 3.9 %copy-start.8 = (s32[128]{0:T(128)S(1)}, s32[128]{0:T(128)}, u32[]{:S(2)}) copy-start(s32[128]{0:T(128)} %param.16) | copy-start | bytes 1540
  206.8 3.9 %copy-start.9 = (s32[128]{0:T(128)S(1)}, s32[128]{0:T(128)}, u32[]{:S(2)}) copy-start(s32[128]{0:T(128)} %param.17) | copy-start | bytes 1540
  206.8 3.9 %copy-start.6 = (f32[64,128]{1,0:T(8,128)S(1)}, f32[64,128]{1,0:T(8,128)}, u32[]{:S(2)}) copy-start(f32[64,128]{1,0:T(8,128)} %get-tuple-element.30) | copy-start | bytes 98308
  206.8 6.7 %copy-start.12 = (bf16[64,128]{1,0:T(8,128)(2,1)S(1)}, bf16[64,128]{1,0:T(8,128)(2,1)}, u32[]{:S(2)}) copy-start(bf16[64,128]{1,0:T(8,128)(2,1)} %get-tuple-element.22) | copy-start | bytes 49156
  206.8 27.4 %all-to-all-start.3 = ((f32[8,8,4,16,128]{4,3,2,1,0:T(8,128)}), f32[8,8,4,16,128]{4,3,2,1,0:T(8,128)S(1)}, u32[]{:S(2)}, u32[]{:S(2)}) async-start(f32[8,8,4,16,128]{4,3,2,1,0:T(8,128)} %get-tuple-element.21), calls=%async_computation.3 | async-start | bytes 4194304 | tf_op jit(solution)/shard_map/all_to_all | solution.py:396
  210.8 4.3 %collective-permute-start.17 = (f32[1,72,128]{2,1,0:T(8,128)S(1)}, f32[1,72,128]{2,1,0:T(8,128)S(1)}, u32[]{:S(2)}, u32[]{:S(2)}) collective-permute-start(f32[1,72,128]{2,1,0:T(8,128)S(1)} %maximum_bitcast_fusion.3), channel_id=1, source_target_pairs={{0,64},{8,72},{16,80},{24,88},{32,96},{40,104},{48,112},{56,120},{... | collective-permute-start | bytes 110600 | tf_op jit(solution)/shard_map/ppermute | solution.py:350
  215.2 32.7 %collective-permute-start.18 = (f32[2,72,128]{2,1,0:T(8,128)S(1)}, f32[2,72,128]{2,1,0:T(8,128)S(1)}, u32[]{:S(2)}, u32[]{:S(2)}) collective-permute-start(f32[2,72,128]{2,1,0:T(8,128)S(1)} %maximum_bitcast_fusion.1), channel_id=1, source_target_pairs={{0,32},{8,40},{16,48},{24,56},{32,0},{40,8},{48,16},{56,24},{64,96... | collective-permute-start | bytes 221192 | tf_op jit(solution)/shard_map/ppermute | solution.py:350
  234.2 1.4 copy-start.1
  235.5 6.7 %copy-start.7 = (f32[64,128]{1,0:T(8,128)S(1)}, f32[64,128]{1,0:T(8,128)}, u32[]{:S(2)}) copy-start(f32[64,128]{1,0:T(8,128)} %get-tuple-element.29) | copy-start | bytes 98308
  235.5 7.6 %copy-start.5 = (bf16[64,64]{1,0:T(8,128)(2,1)S(1)}, bf16[64,64]{1,0:T(8,128)(2,1)}, u32[]{:S(2)}) copy-start(bf16[64,64]{1,0:T(8,128)(2,1)} %w_in_ref.3) | copy-start | bytes 24580
  242.2 28.5 %copy-start.11 = (f32[4,2,8,4096]{3,2,1,0:T(8,128)S(1)}, f32[4,2,8,4096]{3,2,1,0:T(8,128)}, u32[]{:S(2)}) copy-start(f32[4,2,8,4096]{3,2,1,0:T(8,128)} %get-tuple-element.27) | copy-start | bytes 3145732
  243.1 2.8 collective-permute-start.10
  245.8 3.4 %collective-permute-start.11 = (f32[64,128]{1,0:T(8,128)S(1)}, f32[64,128]{1,0:T(8,128)S(1)}, u32[]{:S(2)}, u32[]{:S(2)}) collective-permute-start(f32[64,128]{1,0:T(8,128)S(1)} %add.157), channel_id=1, source_target_pairs={{0,2},{1,3},{2,0},{3,1},{4,6},{5,7},{6,4},{7,5},{8,10},{9,11},{10,... | collective-permute-start | bytes 98312 | tf_op jit(solution)/shard_map/ppermute | solution.py:350
  249.2 4.9 %collective-permute-start.12 = (f32[64,128]{1,0:T(8,128)S(1)}, f32[64,128]{1,0:T(8,128)S(1)}, u32[]{:S(2)}, u32[]{:S(2)}) collective-permute-start(f32[64,128]{1,0:T(8,128)S(1)} %add.158), channel_id=1, source_target_pairs={{0,4},{1,5},{2,6},{3,7},{4,0},{5,1},{6,2},{7,3},{8,12},{9,13},{10,... | collective-permute-start | bytes 98312 | tf_op jit(solution)/shard_map/ppermute | solution.py:350
  251.3 26.5 %copy-start.10 = (f32[4,2,8,4096]{3,2,1,0:T(8,128)S(1)}, f32[4,2,8,4096]{3,2,1,0:T(8,128)}, u32[]{:S(2)}) copy-start(f32[4,2,8,4096]{3,2,1,0:T(8,128)} %get-tuple-element.24) | copy-start | bytes 3145732
  251.3 5.6 %collective-permute-start.19 = (f32[4,72,128]{2,1,0:T(8,128)S(1)}, f32[4,72,128]{2,1,0:T(8,128)S(1)}, u32[]{:S(2)}, u32[]{:S(2)}) collective-permute-start(f32[4,72,128]{2,1,0:T(8,128)S(1)} %bitcast.139), channel_id=1, source_target_pairs={{0,16},{8,24},{16,0},{24,8},{32,48},{40,56},{48,32},{56,40},{64,80... | collective-permute-start | bytes 442376 | tf_op jit(solution)/shard_map/ppermute | solution.py:350
  254.1 4.3 %collective-permute-start.13 = (f32[1,64,128]{2,1,0:T(8,128)S(1)}, f32[1,64,128]{2,1,0:T(8,128)S(1)}, u32[]{:S(2)}, u32[]{:S(2)}) collective-permute-start(f32[1,64,128]{2,1,0:T(8,128)S(1)} %add_bitcast_fusion), channel_id=1, source_target_pairs={{0,64},{8,72},{16,80},{24,88},{32,96},{40,104},{48,112},{56,120},{... | collective-permute-start | bytes 98312 | tf_op jit(solution)/shard_map/ppermute | solution.py:350
  258.5 9.2 %collective-permute-start.14 = (f32[2,64,128]{2,1,0:T(8,128)S(1)}, f32[2,64,128]{2,1,0:T(8,128)S(1)}, u32[]{:S(2)}, u32[]{:S(2)}) collective-permute-start(f32[2,64,128]{2,1,0:T(8,128)S(1)} %maximum_bitcast_fusion.2), channel_id=1, source_target_pairs={{0,32},{8,40},{16,48},{24,56},{32,0},{40,8},{48,16},{56,24},{64,96... | collective-permute-start | bytes 196616 | tf_op jit(solution)/shard_map/ppermute | solution.py:350
  259.8 10.7 %collective-permute-start.20 = (f32[8,72,128]{2,1,0:T(8,128)S(1)}, f32[8,72,128]{2,1,0:T(8,128)S(1)}, u32[]{:S(2)}, u32[]{:S(2)}) collective-permute-start(f32[8,72,128]{2,1,0:T(8,128)S(1)} %bitcast.137), channel_id=1, source_target_pairs={{0,8},{8,0},{16,24},{24,16},{32,40},{40,32},{48,56},{56,48},{64,72... | collective-permute-start | bytes 884744 | tf_op jit(solution)/shard_map/ppermute | solution.py:350
  267.7 6.0 %collective-permute-start.15 = (f32[4,64,128]{2,1,0:T(8,128)S(1)}, f32[4,64,128]{2,1,0:T(8,128)S(1)}, u32[]{:S(2)}, u32[]{:S(2)}) collective-permute-start(f32[4,64,128]{2,1,0:T(8,128)S(1)} %bitcast.140), channel_id=1, source_target_pairs={{0,16},{8,24},{16,0},{24,8},{32,48},{40,56},{48,32},{56,40},{64,80... | collective-permute-start | bytes 393224 | tf_op jit(solution)/shard_map/ppermute | solution.py:350
  270.7 18.6 %copy-start.3 = (f32[4,2,8,4096]{3,2,1,0:T(8,128)S(1)}, f32[4,2,8,4096]{3,2,1,0:T(8,128)}, u32[]{:S(2)}) copy-start(f32[4,2,8,4096]{3,2,1,0:T(8,128)} %get-tuple-element.26) | copy-start | bytes 3145732
  270.7 18.6 %collective-permute-start.5 = (f32[4,2,8,4096]{3,2,1,0:T(8,128)S(1)}, f32[4,2,8,4096]{3,2,1,0:T(8,128)S(1)}, u32[]{:S(2)}, u32[]{:S(2)}) collective-permute-start(f32[4,2,8,4096]{3,2,1,0:T(8,128)S(1)} %copy-done.11), channel_id=1, source_target_pairs={{0,8},{8,0},{16,24},{24,16},{32,40},{40,32},{48,56},{56,48},{64,72... | collective-permute-start | bytes 3145736 | tf_op jit(solution)/shard_map/ppermute | solution.py:350
  273.8 4.5 %collective-permute-start.16 = (f32[8,64,128]{2,1,0:T(8,128)S(1)}, f32[8,64,128]{2,1,0:T(8,128)S(1)}, u32[]{:S(2)}, u32[]{:S(2)}) collective-permute-start(f32[8,64,128]{2,1,0:T(8,128)S(1)} %bitcast.138), channel_id=1, source_target_pairs={{0,8},{8,0},{16,24},{24,16},{32,40},{40,32},{48,56},{56,48},{64,72... | collective-permute-start | bytes 786440 | tf_op jit(solution)/shard_map/ppermute | solution.py:350
  277.8 15.4 %collective-permute-start = (f32[4,2,8,4096]{3,2,1,0:T(8,128)S(1)}, f32[4,2,8,4096]{3,2,1,0:T(8,128)S(1)}, u32[]{:S(2)}, u32[]{:S(2)}) collective-permute-start(f32[4,2,8,4096]{3,2,1,0:T(8,128)S(1)} %copy-done.10), channel_id=1, source_target_pairs={{0,8},{8,0},{16,24},{24,16},{32,40},{40,32},{48,56},{56,48},{64,72... | collective-permute-start | bytes 3145736 | tf_op jit(solution)/shard_map/ppermute | solution.py:350
  278.5 14.7 %copy-start.2 = (f32[4,2,8,4096]{3,2,1,0:T(8,128)S(1)}, f32[4,2,8,4096]{3,2,1,0:T(8,128)}, u32[]{:S(2)}) copy-start(f32[4,2,8,4096]{3,2,1,0:T(8,128)} %get-tuple-element.23) | copy-start | bytes 3145732
  289.5 12.7 %collective-permute-start.8 = (f32[2,8,4096]{2,1,0:T(8,128)S(1)}, f32[2,8,4096]{2,1,0:T(8,128)S(1)}, u32[]{:S(2)}, u32[]{:S(2)}) collective-permute-start(f32[2,8,4096]{2,1,0:T(8,128)S(1)} %get-tuple-element.54), channel_id=1, source_target_pairs={{0,96},{8,104},{16,112},{24,120},{32,0},{40,8},{48,16},{56,24},{64... | collective-permute-start | bytes 786440 | tf_op jit(solution)/shard_map/ppermute | solution.py:369
  292.1 10.1 %collective-permute-start.7 = (f32[2,8,4096]{2,1,0:T(8,128)S(1)}, f32[2,8,4096]{2,1,0:T(8,128)S(1)}, u32[]{:S(2)}, u32[]{:S(2)}) collective-permute-start(f32[2,8,4096]{2,1,0:T(8,128)S(1)} %get-tuple-element.55), channel_id=1, source_target_pairs={{0,64},{8,72},{16,80},{24,88},{32,96},{40,104},{48,112},{56,120},{... | collective-permute-start | bytes 786440 | tf_op jit(solution)/shard_map/ppermute | solution.py:369
  292.6 15.9 %collective-permute-start.6 = (f32[2,8,4096]{2,1,0:T(8,128)S(1)}, f32[2,8,4096]{2,1,0:T(8,128)S(1)}, u32[]{:S(2)}, u32[]{:S(2)}) collective-permute-start(f32[2,8,4096]{2,1,0:T(8,128)S(1)} %get-tuple-element.53), channel_id=1, source_target_pairs={{0,32},{8,40},{16,48},{24,56},{32,64},{40,72},{48,80},{56,88},{64,... | collective-permute-start | bytes 786440 | tf_op jit(solution)/shard_map/ppermute | solution.py:369
  293.3 20.8 %collective-permute-start.3 = (f32[2,8,4096]{2,1,0:T(8,128)S(1)}, f32[2,8,4096]{2,1,0:T(8,128)S(1)}, u32[]{:S(2)}, u32[]{:S(2)}) collective-permute-start(f32[2,8,4096]{2,1,0:T(8,128)S(1)} %get-tuple-element.51), channel_id=1, source_target_pairs={{0,96},{8,104},{16,112},{24,120},{32,0},{40,8},{48,16},{56,24},{64... | collective-permute-start | bytes 786440 | tf_op jit(solution)/shard_map/ppermute | solution.py:369
  295.5 18.7 %collective-permute-start.2 = (f32[2,8,4096]{2,1,0:T(8,128)S(1)}, f32[2,8,4096]{2,1,0:T(8,128)S(1)}, u32[]{:S(2)}, u32[]{:S(2)}) collective-permute-start(f32[2,8,4096]{2,1,0:T(8,128)S(1)} %get-tuple-element.52), channel_id=1, source_target_pairs={{0,64},{8,72},{16,80},{24,88},{32,96},{40,104},{48,112},{56,120},{... | collective-permute-start | bytes 786440 | tf_op jit(solution)/shard_map/ppermute | solution.py:369
  302.3 16.4 %collective-permute-start.1 = (f32[2,8,4096]{2,1,0:T(8,128)S(1)}, f32[2,8,4096]{2,1,0:T(8,128)S(1)}, u32[]{:S(2)}, u32[]{:S(2)}) collective-permute-start(f32[2,8,4096]{2,1,0:T(8,128)S(1)} %get-tuple-element.50), channel_id=1, source_target_pairs={{0,32},{8,40},{16,48},{24,56},{32,64},{40,72},{48,80},{56,88},{64,... | collective-permute-start | bytes 786440 | tf_op jit(solution)/shard_map/ppermute | solution.py:369
  308.6 12.8 %collective-permute-start.9 = (f32[2,4,4096]{2,1,0:T(4,128)S(1)}, f32[2,4,4096]{2,1,0:T(4,128)S(1)}, u32[]{:S(2)}, u32[]{:S(2)}) collective-permute-start(f32[2,4,4096]{2,1,0:T(4,128)S(1)} %slice.75), channel_id=1, source_target_pairs={{0,16},{8,24},{16,0},{24,8},{32,48},{40,56},{48,32},{56,40},{64,80... | collective-permute-start | bytes 393224 | tf_op jit(solution)/shard_map/ppermute | solution.py:350
  318.7 6.0 %collective-permute-start.4 = (f32[2,4,4096]{2,1,0:T(4,128)S(1)}, f32[2,4,4096]{2,1,0:T(4,128)S(1)}, u32[]{:S(2)}, u32[]{:S(2)}) collective-permute-start(f32[2,4,4096]{2,1,0:T(4,128)S(1)} %slice.69), channel_id=1, source_target_pairs={{0,16},{8,24},{16,0},{24,8},{32,48},{40,56},{48,32},{56,40},{64,80... | collective-permute-start | bytes 393224 | tf_op jit(solution)/shard_map/ppermute | solution.py:350
